TPU v7x, 512 devices: a whole 4x4x16 slice. The times are simulated.
512 devices in a mesh: gx: 32 (over y_hi, z), gy: 4 (over x), gz: 4 (over y_lo, core).
Axes of the slice: x: 4, y: 4 (y_hi: 2, y_lo: 2; y = y_hi * 2 + y_lo), z: 16, core: 2. Of those that a mesh axis runs over, the one named last changes fastest.
Arguments:
- fields: float32 [12, 256, 32, 512], P(None, 'gx', 'gy', 'gz'), as said below
- reacting: int32 [256, 32, 512], P('gx', 'gy', 'gz'), may hold values from 0 to 1, as said below
- panel_map: int32 [2, 256, 512], P(None, 'gx', 'gz'), may hold values from 0 to 4095, as said below
- layer_one: bfloat16 [1600, 12], replicated, may hold values from -4 to 4
- layer_two: bfloat16 [800, 1600], replicated, may hold values from -0.21875 to 0.21875
- layer_three: bfloat16 [400, 800], replicated, may hold values from -0.3125 to 0.3125
- layer_four: bfloat16 [12, 400], replicated, may hold values from -0.3125 to 0.3125
Outputs:
- new_fields: float32 [12, 256, 32, 512], P(None, 'gx', 'gy', 'gz')
- impulse: float32 [4096], P(('gx', 'gy', 'gz'))
Inputs may be any that keep to these rules, and one draw needn't show every extreme that they name: `fields`: component 0 (density) lies between 0.3 and 3.3; the velocities (components 1 to 3 over component 0) between -1.2 and 1.2; the pressure 0.4 (component 4 - |momentum|^2 / (2 density)) between 0.3 and 5; components 5 to 11 are 0.01 to 0.14 times component 0. Each device's aligned block of 8 x 8 x 128 cells holds at most 256 reacting cells. The blocks that share their ranges along the second and third dimensions hold exactly 64 reacting cells each on average, and one in eight of them, and at least one, hold exactly 256. `panel_map`: every panel is a patch of 8 x 8 cells of one wall, shifted by 4 cells along the first dimension and closed around it; panels are numbered in a random order and each number is used once.
All inputs are finite; a program needn't handle non-finite values.
Results may differ from a plain program's by a relative error of at most 0.0014.
Values may be sent and summed in bfloat16 or wider, within the bound.
A program may use at most 64 MiB of HBM per device.

v0:
```python
import jax
import jax.numpy as jnp
from jax import lax
from jax.sharding import PartitionSpec as P

BAL = 64
COMPS = 12
PATCH = 8
HEAT_RATIO = 1.4
TIME_STEP = 0.1
CHEM_STEP = 0.25
WENO_EPS = 1e-06


def extended(array, sides, width):
    for axis, dim in sides:
        size, length = (lax.axis_size(axis), array.shape[dim])
        up = [(i, (i + 1) % size) for i in range(size - 1)]
        down = [(j, i) for i, j in up]
        last = lax.slice_in_dim(array, length - width, length, axis=dim)
        initial = lax.slice_in_dim(array, 0, width, axis=dim)
        before = lax.ppermute(last, axis, up)
        after = lax.ppermute(initial, axis, down)
        array = jnp.concatenate([before, array, after], axis=dim)
    return array


def take_slab(array_in, begin_at, length_of, flux_axis):
    return lax.slice_in_dim(array_in, begin_at, begin_at + length_of, axis=flux_axis)


def weno_face(upwind_two, upwind_one, center, downwind_one, downwind_two):
    cand_zero = (2.0 * upwind_two - 7.0 * upwind_one + 11.0 * center) / 6.0
    cand_one = (-upwind_one + 5.0 * center + 2.0 * downwind_one) / 6.0
    cand_two = (2.0 * center + 5.0 * downwind_one - downwind_two) / 6.0
    smooth_zero = (
        13.0 / 12.0 * (upwind_two - 2.0 * upwind_one + center) ** 2
        + 0.25 * (upwind_two - 4.0 * upwind_one + 3.0 * center) ** 2
    )
    smooth_one = (
        13.0 / 12.0 * (upwind_one - 2.0 * center + downwind_one) ** 2
        + 0.25 * (upwind_one - downwind_one) ** 2
    )
    smooth_two = (
        13.0 / 12.0 * (center - 2.0 * downwind_one + downwind_two) ** 2
        + 0.25 * (3.0 * center - 4.0 * downwind_one + downwind_two) ** 2
    )
    weight_zero = 0.1 / (WENO_EPS + smooth_zero) ** 2
    weight_one = 0.6 / (WENO_EPS + smooth_one) ** 2
    weight_two = 0.3 / (WENO_EPS + smooth_two) ** 2
    weight_sum = weight_zero + weight_one + weight_two
    return (weight_zero * cand_zero + weight_one * cand_one + weight_two * cand_two) / weight_sum


def to_recon(fields):
    density = fields[0]
    velocity = fields[1:4] / density[None]
    pressure = (HEAT_RATIO - 1.0) * (
        fields[4] - 0.5 * density * jnp.sum(velocity * velocity, axis=0)
    )
    fractions = fields[5:] / density[None]
    return jnp.concatenate(
        [jnp.log(density)[None], velocity, jnp.log(pressure)[None], fractions], axis=0
    )


def normal_of(normal, ndims):
    return (jnp.arange(3) == normal).reshape((3,) + (1,) * (ndims - 1))


def side_terms(recon, normal):
    density = jnp.exp(recon[0])
    velocity = recon[1:4]
    pressure = jnp.exp(recon[4])
    fractions = recon[5:]
    speed_n = velocity[normal]
    energy = pressure / (HEAT_RATIO - 1.0) + 0.5 * density * jnp.sum(velocity * velocity, axis=0)
    conserved = jnp.concatenate(
        [density[None], density[None] * velocity, energy[None], density[None] * fractions], axis=0
    )
    mass_flux = density * speed_n
    normal_mask = normal_of(normal, recon.ndim)
    momentum_flux = mass_flux[None] * velocity + jnp.where(normal_mask, pressure[None], 0.0)
    flux_terms = jnp.concatenate(
        [
            mass_flux[None],
            momentum_flux,
            ((energy + pressure) * speed_n)[None],
            mass_flux[None] * fractions,
        ],
        axis=0,
    )
    sound_speed = jnp.sqrt(HEAT_RATIO * pressure / density)
    return (
        density,
        velocity,
        pressure,
        fractions,
        energy,
        conserved,
        flux_terms,
        speed_n,
        sound_speed,
    )


def star_state(
    density, velocity, pressure, fractions, energy, speed_n, wave_speed, contact, normal_mask
):
    relative = wave_speed - speed_n
    factor = density * relative / (wave_speed - contact)
    star_velocity = jnp.where(normal_mask, contact[None], velocity)
    star_energy = energy / density + (contact - speed_n) * (
        contact + pressure / (density * relative)
    )
    return jnp.concatenate(
        [
            factor[None],
            factor[None] * star_velocity,
            (factor * star_energy)[None],
            factor[None] * fractions,
        ],
        axis=0,
    )


def hllc_flux(left_recon, right_recon, normal):
    (
        left_density,
        left_velocity,
        left_pressure,
        left_fractions,
        left_energy,
        left_cons,
        left_flux,
        left_speed,
        left_sound,
    ) = side_terms(left_recon, normal)
    (
        right_density,
        right_velocity,
        right_pressure,
        right_fractions,
        right_energy,
        right_cons,
        right_flux,
        right_speed,
        right_sound,
    ) = side_terms(right_recon, normal)
    wave_left = jnp.minimum(left_speed - left_sound, right_speed - right_sound)
    wave_right = jnp.maximum(left_speed + left_sound, right_speed + right_sound)
    left_rel = wave_left - left_speed
    right_rel = wave_right - right_speed
    contact = (
        right_pressure
        - left_pressure
        + left_density * left_speed * left_rel
        - right_density * right_speed * right_rel
    ) / (left_density * left_rel - right_density * right_rel)
    normal_mask = normal_of(normal, left_recon.ndim)
    star_left = star_state(
        left_density,
        left_velocity,
        left_pressure,
        left_fractions,
        left_energy,
        left_speed,
        wave_left,
        contact,
        normal_mask,
    )
    star_right = star_state(
        right_density,
        right_velocity,
        right_pressure,
        right_fractions,
        right_energy,
        right_speed,
        wave_right,
        contact,
        normal_mask,
    )
    left_star_flux = left_flux + wave_left[None] * (star_left - left_cons)
    right_star_flux = right_flux + wave_right[None] * (star_right - right_cons)
    return jnp.where(
        wave_left[None] >= 0,
        left_flux,
        jnp.where(
            contact[None] >= 0,
            left_star_flux,
            jnp.where(wave_right[None] > 0, right_star_flux, right_flux),
        ),
    )


def face_flux(padded, normal):
    flux_axis = normal + 1
    face_count = padded.shape[flux_axis] - 5
    stencil = [take_slab(padded, offset, face_count, flux_axis) for offset in range(6)]
    left_state = weno_face(stencil[0], stencil[1], stencil[2], stencil[3], stencil[4])
    right_state = weno_face(stencil[5], stencil[4], stencil[3], stencil[2], stencil[1])
    return hllc_flux(left_state, right_state, normal)


def mirror_walls(padded, normal, at_first, at_last):
    flux_axis = normal + 1
    cell_count = padded.shape[flux_axis] - 6
    flip_sign = (
        jnp.where(jnp.arange(padded.shape[0]) == 1 + normal, -1.0, 1.0)
        .astype(padded.dtype)
        .reshape((-1, 1, 1, 1))
    )
    ghost_low = jnp.flip(take_slab(padded, 3, 3, flux_axis), flux_axis) * flip_sign
    ghost_high = jnp.flip(take_slab(padded, cell_count, 3, flux_axis), flux_axis) * flip_sign
    low_side = jnp.where(at_first, ghost_low, take_slab(padded, 0, 3, flux_axis))
    high_side = jnp.where(at_last, ghost_high, take_slab(padded, cell_count + 3, 3, flux_axis))
    return jnp.concatenate(
        [low_side, take_slab(padded, 3, cell_count, flux_axis), high_side], axis=flux_axis
    )


def chem_rates(features, layer_one, layer_two, layer_three, layer_four):
    hidden_one = jax.nn.gelu(
        jnp.dot(layer_one, features, preferred_element_type=jnp.float32)
    ).astype(jnp.bfloat16)
    hidden_two = jax.nn.gelu(
        jnp.dot(layer_two, hidden_one, preferred_element_type=jnp.float32)
    ).astype(jnp.bfloat16)
    hidden_three = jax.nn.gelu(
        jnp.dot(layer_three, hidden_two, preferred_element_type=jnp.float32)
    ).astype(jnp.bfloat16)
    return jnp.dot(layer_four, hidden_three, preferred_element_type=jnp.float32).astype(
        jnp.bfloat16
    )


def body(fields, reacting, panel_map, layer_one, layer_two, layer_three, layer_four):
    recon_fields = to_recon(fields)
    gx_count = lax.axis_size("gx")
    gy_count = lax.axis_size("gy")
    gz_count = lax.axis_size("gz")
    at_first = (lax.axis_index("gx") == 0, lax.axis_index("gy") == 0, lax.axis_index("gz") == 0)
    at_last = (
        lax.axis_index("gx") == gx_count - 1,
        lax.axis_index("gy") == gy_count - 1,
        lax.axis_index("gz") == gz_count - 1,
    )
    padded = extended(recon_fields, (("gx", 1), ("gy", 2), ("gz", 3)), 3)
    line_fields = (padded[:, :, 3:-3, 3:-3], padded[:, 3:-3, :, 3:-3], padded[:, 3:-3, 3:-3, :])
    update = jnp.zeros_like(fields)
    push_low = None
    push_high = None
    for normal in range(3):
        line_block = mirror_walls(line_fields[normal], normal, at_first[normal], at_last[normal])
        face_fluxes = face_flux(line_block, normal)
        cell_count = face_fluxes.shape[normal + 1] - 1
        change = take_slab(face_fluxes, 1, cell_count, normal + 1) - take_slab(
            face_fluxes, 0, cell_count, normal + 1
        )
        update = update + change
        if normal == 1:
            push_low = face_fluxes[2, :, 0, :]
            push_high = face_fluxes[2, :, cell_count, :]
    cell_total = reacting.size
    react_flags = reacting.reshape(cell_total)
    capacity = BAL * min(4, gx_count)
    per_peer = capacity // gx_count
    row_rank = jnp.cumsum(react_flags) - 1
    slot_index = jnp.where(
        react_flags == 1, row_rank % gx_count * per_peer + row_rank // gx_count, capacity
    )
    flat_features = recon_fields.reshape(COMPS, cell_total).astype(jnp.bfloat16)
    packed = (
        jnp.zeros((COMPS, capacity), jnp.bfloat16).at[:, slot_index].set(flat_features, mode="drop")
    )
    rate_packed = chem_rates(packed, layer_one, layer_two, layer_three, layer_four)
    gathered = rate_packed[:, jnp.where(react_flags == 1, slot_index, 0)]
    source = jnp.where(react_flags[None, :] == 1, gathered.astype(jnp.float32), 0.0).reshape(
        fields.shape
    )
    new_fields = fields - TIME_STEP * update + CHEM_STEP * source
    on_low = lax.axis_index("gy") == 0
    on_high = lax.axis_index("gy") == gy_count - 1
    push_values = jnp.concatenate(
        [
            jnp.where(on_low, push_low, 0.0).reshape(-1),
            jnp.where(on_high, push_high, 0.0).reshape(-1),
        ]
    )
    panel_ids = jnp.concatenate([panel_map[0].reshape(-1), panel_map[1].reshape(-1)])
    panels_all = 2 * (fields.shape[1] * gx_count // PATCH) * (fields.shape[3] * gz_count // PATCH)
    own_panels = panels_all // (gx_count * gy_count * gz_count)
    partial_loads = jax.ops.segment_sum(push_values, panel_ids, num_segments=panels_all)
    totals = lax.psum(partial_loads, ("gx", "gy", "gz"))
    flat_index = (
        lax.axis_index("gx") * gy_count + lax.axis_index("gy")
    ) * gz_count + lax.axis_index("gz")
    result = lax.dynamic_slice_in_dim(totals, flat_index * own_panels, own_panels)
    impulse = result / float(PATCH * PATCH)
    return (new_fields, impulse)


def solution(mesh):
    return jax.shard_map(
        body,
        mesh=mesh,
        in_specs=(
            P(None, "gx", "gy", "gz"),
            P("gx", "gy", "gz"),
            P(None, "gx", "gz"),
            P(),
            P(),
            P(),
            P(),
        ),
        out_specs=(P(None, "gx", "gy", "gz"), P(("gx", "gy", "gz"))),
        check_vma=False,
    )
```

profile of v0, /device:TPU:1, one launch (start us, length us, event | category | flops | bytes accessed | tf_op | source)
XLA Modules:
  0.0 275.4 jit_solution(14904916895954684997)
XLA Ops:
  0.6 0.9 convert_bitcast_fusion.3
  1.6 0.9 convert_bitcast_fusion.1
  2.5 1.0 convert_bitcast_fusion
  3.5 0.8 convert_bitcast_fusion.2
  4.3 0.8 fusion.173
  5.1 5.0 %collective-permute-start = (f32[12,3,8,128]{3,2,1,0:T(8,128)}, f32[12,3,8,128]{3,2,1,0:T(8,128)}, u32[]{:S(2)}, u32[]{:S(2)}) collective-permute-start(f32[12,3,8,128]{3,2,1,0:T(8,128)} %get-tuple-element.138), channel_id=1, source_target_pairs={{0,16},{16,32},{32,48},{48,64},{64,80},{80,96},{96,112},{112,128},... | collective-permute-start | bytes 442376 | tf_op jit(solution)/shard_map/ppermute | solution.py:22
  10.2 1.3 collective-permute-start.1
  11.4 0.9 fusion.171
  12.3 0.5 iota_compare_fusion.1
  12.8 0.5 compare_select_fusion.7
  13.3 0.6 iota_compare_fusion.2
  13.9 0.9 fusion.172
  14.8 0.5 compare_select_fusion.5
  15.5 0.9 maximum_bitcast_fusion
  16.4 2.7 copy.63
  19.4 0.7 slice.440
  20.1 0.9 reduce-window.12
  21.6 21.7 %scatter_custom_fusion = bf16[12,256]{0,1:T(8,128)(2,1)} fusion(s32[8192]{0:T(1024)S(1)} %bitcast.214, bf16[8192,12]{1,0:T(8,128)(2,1)} %copy.63, bf16[]{:T(256)} %constant.78.clone.1), kind=kCustom, calls=%fused_computation.316 | custom fusion | bytes 6656 | tf_op jit(solution)/shard_map/scatter | solution.py:274
  43.3 3.2 %fusion.16 = bf16[800,256]{1,0:T(8,128)(2,1)} fusion(bf16[800,1600]{1,0:T(8,128)(2,1)S(1)} %copy-done, bf16[12,256]{0,1:T(8,128)(2,1)} %scatter_custom_fusion, bf16[1600,12]{0,1:T(8,128)(2,1)} %param.10), kind=kOutput, calls=%fused_computation.28 | convolution fusion | flops 670720000 | bytes 3014144 | tf_op jit(solution)/shard_map/dot_general | solution.py:227
  46.5 1.8 fusion.8
  48.2 0.6 iota_compare_fusion
  48.8 1.8 rev.23
  50.6 1.8 rev.24
  52.4 1.9 rev.25
  54.3 0.9 rev.26
  55.4 29.4 %gather_fusion = bf16[8192,12]{1,0:T(8,128)(2,1)} fusion(bf16[12,256]{0,1:T(8,128)(2,1)S(1)} %copy.64, s32[8192]{0:T(1024)S(1)} %broadcast_clamp_fusion), kind=kCustom, calls=%fused_computation | custom fusion | bytes 425984 | tf_op jit(solution)/shard_map/gather | solution.py:277
  84.8 3.8 %convert_element_type.31 = f32[8192,12]{1,0:T(8,128)} convert(bf16[8192,12]{1,0:T(8,128)(2,1)} %gather_fusion) | non-fusion elementwise | flops 98304 | bytes 589824 | tf_op jit(solution)/shard_map/convert_element_type | solution.py:278
  88.6 3.6 %copy.66 = f32[12,8,8,128]{3,2,1,0:T(8,128)} copy(f32[12,8,8,128]{0,3,2,1:T(8,128)} %bitcast.175) | data formatting | bytes 786432 | tf_op jit(solution)/shard_map/convert_element_type | solution.py:278
  92.1 0.6 pad_add_fusion
  92.8 1.2 multiply_select_fusion.2
  94.0 1.9 add_divide_fusion.2
  96.0 1.0 pad_maximum_fusion.5
  97.2 3.1 %collective-permute-start.2 = (f32[12,14,3,128]{3,1,2,0:T(8,128)S(1)}, f32[12,14,3,128]{3,1,2,0:T(8,128)S(1)}, u32[]{:S(2)}, u32[]{:S(2)}) collective-permute-start(f32[12,14,3,128]{3,1,2,0:T(8,128)S(1)} %copy.53), channel_id=1, source_target_pairs={{0,4},{4,8},{8,12},{1,5},{5,9},{9,13},{2,6},{6,10},{10,14},{3,7},{... | collective-permute-start | bytes 774152 | tf_op jit(solution)/shard_map/ppermute | solution.py:22
  100.4 1.5 collective-permute-start.3
  102.2 0.4 copy-done.14
  103.0 1.9 collective-permute-done.2
  105.1 3.7 %collective-permute-done.3 = f32[12,14,3,128]{3,1,2,0:T(8,128)S(1)} collective-permute-done((f32[12,14,3,128]{3,1,2,0:T(8,128)S(1)}, f32[12,14,3,128]{3,1,2,0:T(8,128)S(1)}, u32[]{:S(2)}, u32[]{:S(2)}) %collective-permute-start.3) | collective-permute-done | bytes 258080 | tf_op jit(solution)/shard_map/ppermute | solution.py:23
  109.1 0.5 copy-done.4
  109.9 3.6 %add_divide_fusion.1 = (f32[12,8,9,128]{3,2,1,0:T(8,128)S(1)}, f32[12,8,9,128]{3,2,1,0:T(8,128)S(1)}) fusion(f32[12,8,11,128]{3,2,1,0:T(8,128)S(1)} %get-tuple-element.130, f32[12,8,11,128]{3,2,1,0:T(8,128)S(1)} %get-tuple-element.131), kind=kLoop, calls=%fused_computation.80 | loop fusion | flops 13713408 | bytes 3538944 | tf_op jit(solution)/shard_map/div | solution.py:52
  114.0 0.3 slice_multiply_fusion.6
  114.3 0.3 copy-done.13
  114.8 0.5 fusion.22
  115.4 0.9 copy-done.1
  116.2 14.0 %scatter_custom_fusion.1 = f32[4096]{0:T(1024)S(1)} fusion(s32[2048]{0:T(1024)} %pad_add_fusion, f32[2048]{0:T(1024)S(1)} %pad_maximum_fusion.9, f32[]{:T(128)} %constant.54.clone.1), kind=kCustom, calls=%fused_computation.342 | custom fusion | flops 2048 | bytes 16896 | tf_op jit(solution)/shard_map/scatter-add | solution.py:293
  130.3 111.0 %psum.7 = f32[4096]{0:T(1024)S(1)} all-reduce(f32[4096]{0:T(1024)S(1)} %scatter_custom_fusion.1), channel_id=1, replica_groups=mesh['gx'=32,'gy'=4,'gz'=4] {'gx','gy','gz'}, use_global_device_ids=true, to_apply=%region_11.12 | all-reduce | flops 4096 | bytes 32768 | tf_op jit(solution)/shard_map/psum | solution.py:294
  241.3 1.5 pad_maximum_fusion
  242.8 2.0 fusion.169
  244.8 3.4 %copy.59 = f32[12,14,14,3]{2,1,3,0:T(8,128)} copy(f32[12,14,14,3]{3,2,1,0:T(8,128)} %get-tuple-element.58) | data formatting | bytes 56448 | tf_op jit(solution)/shard_map/slice | solution.py:20
  248.2 2.1 collective-permute-start.4
  250.3 3.4 %copy.61 = f32[12,14,14,3]{2,1,3,0:T(8,128)} copy(f32[12,14,14,3]{3,2,1,0:T(8,128)} %get-tuple-element.57) | data formatting | bytes 56448 | tf_op jit(solution)/shard_map/slice | solution.py:21
  253.7 2.9 %collective-permute-start.5 = (f32[12,14,14,3]{2,1,3,0:T(8,128)}, f32[12,14,14,3]{2,1,3,0:T(8,128)}, u32[]{:S(2)}, u32[]{:S(2)}) collective-permute-start(f32[12,14,14,3]{2,1,3,0:T(8,128)} %copy.61), channel_id=1, source_target_pairs={{1,0},{2,1},{3,2},{5,4},{6,5},{7,6},{9,8},{10,9},{11,10},{13,12},{... | collective-permute-start | bytes 84680 | tf_op jit(solution)/shard_map/ppermute | solution.py:23
  256.6 0.6 dynamic-slice_multiply_fusion
  257.2 1.7 slice.418
  258.9 2.3 copy.67
  261.2 0.9 collective-permute-done.5
  262.1 1.7 slice.424
  263.8 2.3 copy.68
  266.1 1.5 multiply_select_fusion
  267.8 3.9 %add_divide_fusion = (f32[12,8,8,129]{3,2,1,0:T(8,128)S(1)}, f32[12,8,8,129]{3,2,1,0:T(8,128)S(1)}) fusion(f32[12,8,8,131]{3,2,1,0:T(8,128)S(1)} %get-tuple-element.134, f32[12,8,8,131]{3,2,1,0:T(8,128)S(1)} %get-tuple-element.135), kind=kLoop, calls=%fused_computation.53 | loop fusion | flops 12284928 | bytes 3170304 | tf_op jit(solution)/shard_map/div | solution.py:52
  272.3 0.3 slice_multiply_fusion
  272.6 0.3 copy-done.11
  273.1 0.5 fusion.24
  273.7 0.6 copy-done.2
  274.4 1.0 fusion.113
  (87 shorter events, 4.6 us)
Async XLA Ops:
  0.6 42.6 %copy-start = (bf16[800,1600]{1,0:T(8,128)(2,1)S(1)}, bf16[800,1600]{1,0:T(8,128)(2,1)}, u32[]{:S(2)}) copy-start(bf16[800,1600]{1,0:T(8,128)(2,1)} %param.11) | copy-start | bytes 7680004
  4.3 11.0 %copy-start.10 = (s32[2,8,128]{2,1,0:T(8,128)S(1)}, s32[2,8,128]{2,1,0:T(8,128)}, u32[]{:S(2)}) copy-start(s32[2,8,128]{2,1,0:T(8,128)} %param.9) | copy-start | bytes 24580
  5.1 87.6 %collective-permute-start = (f32[12,3,8,128]{3,2,1,0:T(8,128)}, f32[12,3,8,128]{3,2,1,0:T(8,128)}, u32[]{:S(2)}, u32[]{:S(2)}) collective-permute-start(f32[12,3,8,128]{3,2,1,0:T(8,128)} %get-tuple-element.138), channel_id=1, source_target_pairs={{0,16},{16,32},{32,48},{48,64},{64,80},{80,96},{96,112},{112,128},... | collective-permute-start | bytes 442376 | tf_op jit(solution)/shard_map/ppermute | solution.py:22
  10.2 82.6 %collective-permute-start.1 = (f32[12,3,8,128]{3,2,1,0:T(8,128)}, f32[12,3,8,128]{3,2,1,0:T(8,128)}, u32[]{:S(2)}, u32[]{:S(2)}) collective-permute-start(f32[12,3,8,128]{3,2,1,0:T(8,128)} %get-tuple-element.139), channel_id=1, source_target_pairs={{16,0},{32,16},{48,32},{64,48},{80,64},{96,80},{112,96},{128,112},... | collective-permute-start | bytes 442376 | tf_op jit(solution)/shard_map/ppermute | solution.py:23
  15.3 3.8 %copy-start.9 = (s32[8,8,128]{2,1,0:T(8,128)S(1)}, s32[8,8,128]{2,1,0:T(8,128)}, u32[]{:S(2)}) copy-start(s32[8,8,128]{2,1,0:T(8,128)} %param.8) | copy-start | bytes 98308
  43.3 3.2 %copy-start.16 = (bf16[12,400]{1,0:T(8,128)(2,1)S(1)}, bf16[12,400]{1,0:T(8,128)(2,1)}, u32[]{:S(2)}) copy-start(bf16[12,400]{1,0:T(8,128)(2,1)} %param.13) | copy-start | bytes 28804
  88.6 4.2 %copy-start.15 = (f32[12]{0:T(128)S(1)}, f32[12]{0:T(128)}, u32[]{:S(2)}) copy-start(f32[12]{0:T(128)} %compare_select_fusion.7) | copy-start | bytes 148
  97.2 7.7 %collective-permute-start.2 = (f32[12,14,3,128]{3,1,2,0:T(8,128)S(1)}, f32[12,14,3,128]{3,1,2,0:T(8,128)S(1)}, u32[]{:S(2)}, u32[]{:S(2)}) collective-permute-start(f32[12,14,3,128]{3,1,2,0:T(8,128)S(1)} %copy.53), channel_id=1, source_target_pairs={{0,4},{4,8},{8,12},{1,5},{5,9},{9,13},{2,6},{6,10},{10,14},{3,7},{... | collective-permute-start | bytes 774152 | tf_op jit(solution)/shard_map/ppermute | solution.py:22
  100.4 8.4 %collective-permute-start.3 = (f32[12,14,3,128]{3,1,2,0:T(8,128)S(1)}, f32[12,14,3,128]{3,1,2,0:T(8,128)S(1)}, u32[]{:S(2)}, u32[]{:S(2)}) collective-permute-start(f32[12,14,3,128]{3,1,2,0:T(8,128)S(1)} %copy.55), channel_id=1, source_target_pairs={{4,0},{8,4},{12,8},{5,1},{9,5},{13,9},{6,2},{10,6},{14,10},{7,3},{... | collective-permute-start | bytes 774152 | tf_op jit(solution)/shard_map/ppermute | solution.py:23
  102.0 0.7 copy-start.14
  102.7 6.2 %copy-start.7 = (f32[12,8,3,128]{3,2,1,0:T(4,128)S(1)}, f32[12,8,3,128]{3,2,1,0:T(4,128)}, u32[]{:S(2)}) copy-start(f32[12,8,3,128]{3,2,1,0:T(4,128)} %rev.23) | copy-start | bytes 442372
  102.7 6.2 %copy-start.8 = (f32[12,8,3,128]{3,2,1,0:T(4,128)S(1)}, f32[12,8,3,128]{3,2,1,0:T(4,128)}, u32[]{:S(2)}) copy-start(f32[12,8,3,128]{3,2,1,0:T(4,128)} %rev.24) | copy-start | bytes 442372
  105.0 4.1 %copy-start.3 = (f32[12,14,3,128]{3,2,1,0:T(4,128)}, f32[12,14,3,128]{3,2,1,0:T(4,128)S(1)}, u32[]{:S(2)}) copy-start(f32[12,14,3,128]{3,2,1,0:T(4,128)S(1)} %copy.54) | copy-start | bytes 774148
  109.0 0.7 copy-start.4
  114.0 0.7 copy-start.13
  115.3 0.9 copy-start.1
  248.2 9.0 %collective-permute-start.4 = (f32[12,14,14,3]{2,1,3,0:T(8,128)}, f32[12,14,14,3]{2,1,3,0:T(8,128)}, u32[]{:S(2)}, u32[]{:S(2)}) collective-permute-start(f32[12,14,14,3]{2,1,3,0:T(8,128)} %copy.59), channel_id=1, source_target_pairs={{0,1},{1,2},{2,3},{4,5},{5,6},{6,7},{8,9},{9,10},{10,11},{12,13},{... | collective-permute-start | bytes 84680 | tf_op jit(solution)/shard_map/ppermute | solution.py:22
  250.3 15.7 %copy-start.12 = (f32[12]{0:T(128)S(1)}, f32[12]{0:T(128)}, u32[]{:S(2)}) copy-start(f32[12]{0:T(128)} %compare_select_fusion.5) | copy-start | bytes 148
  253.7 8.3 %collective-permute-start.5 = (f32[12,14,14,3]{2,1,3,0:T(8,128)}, f32[12,14,14,3]{2,1,3,0:T(8,128)}, u32[]{:S(2)}, u32[]{:S(2)}) collective-permute-start(f32[12,14,14,3]{2,1,3,0:T(8,128)} %copy.61), channel_id=1, source_target_pairs={{1,0},{2,1},{3,2},{5,4},{6,5},{7,6},{9,8},{10,9},{11,10},{13,12},{... | collective-permute-start | bytes 84680 | tf_op jit(solution)/shard_map/ppermute | solution.py:23
  272.3 0.7 copy-start.11
  273.1 1.1 copy-start.2
  273.1 1.2 copy-start.5
  273.1 1.3 copy-start.6
where the time goes:
time: 276 us; the launch traced here: 275 us
  blocking collectives  111 us (40%)
  local copies, waits for them, and re-layouts  87.9 us (32%)
  other arithmetic  47.9 us (17%)
  starting transfers between devices  15.9 us (6%)
  waiting for transfers between devices  6.54 us (2%)
  matrix products  4.97 us (2%)
    psum x1, blocking collectives, body(): totals = lax.psum(partial_loads, ('gx', 'gy', 'gz'))  111 us
    gather x1, local copies, waits for them, and re-layouts, body(): gathered = rate_packed[:, jnp.where(react_flags == 1, slot_index, 0)]  29.4 us
    scatter x1, local copies, waits for them, and re-layouts, body(): jnp.zeros((COMPS, capacity), jnp.bfloat16).at[:, slot_index]  21.7 us
    scatter-add x1, other arithmetic, body(): jax.ops.segment_sum(push_values, panel_ids, num_segments=panels_all)  14 us
    ppermute x3, starting transfers between devices, extended(): before = lax.ppermute(last, axis, up)  10.3 us
    div x3, other arithmetic, weno_face(): (weight_zero * cand_zero + weight_one * cand_one + weight_two * cand_two)...  9.43 us
    unnamed x38, local copies, waits for them, and re-layouts  7.97 us
    ppermute x3, starting transfers between devices, extended(): after = lax.ppermute(initial, axis, down)  5.61 us
  transfers between devices with their start and end apart: 6, of which 3 were waited for; matrix products, arithmetic and copies ran while one was open for 33% of the time, Pallas kernels for 0%

commit v1 on v0

--- a/solution.py
+++ b/solution.py
@@ -291,7 +291,7 @@
     panels_all = 2 * (fields.shape[1] * gx_count // PATCH) * (fields.shape[3] * gz_count // PATCH)
     own_panels = panels_all // (gx_count * gy_count * gz_count)
     partial_loads = jax.ops.segment_sum(push_values, panel_ids, num_segments=panels_all)
-    totals = lax.psum(partial_loads, ("gx", "gy", "gz"))
+    totals = lax.psum(lax.psum(partial_loads, ("gy", "gz")), "gx")
     flat_index = (
         lax.axis_index("gx") * gy_count + lax.axis_index("gy")
     ) * gz_count + lax.axis_index("gz")

time: 276 us -> 374 us (1.36)
  blocking collectives: 111 us -> 178 us
  starting transfers between devices: 15.9 us -> 47.2 us
    psum x1 -> x2, blocking collectives: 111 us -> 178 us  [body(): totals = lax.psum(lax.psum(partial_loads, ('gy', 'gz')), 'gx')]
    ppermute x3, starting transfers between devices: 10.3 us -> 39.1 us  [extended(): before = lax.ppermute(last, axis, up)]
  transfers between devices with their start and end apart: 6 -> 6, of which waited for: 3 -> 2; matrix products, arithmetic and copies ran while one was open for 33% -> 24% of each run, Pallas kernels for 0% -> 0%
where the time goes in v1:
time: 374 us; the launch traced here: 373 us
  blocking collectives  178 us (48%)
  local copies, waits for them, and re-layouts  87.6 us (23%)
  other arithmetic  47.9 us (13%)
  starting transfers between devices  47.2 us (13%)
  waiting for transfers between devices  5.66 us (2%)
  matrix products  4.96 us (1%)
    psum x2, blocking collectives, body(): totals = lax.psum(lax.psum(partial_loads, ('gy', 'gz')), 'gx')  178 us
    ppermute x3, starting transfers between devices, extended(): before = lax.ppermute(last, axis, up)  39.1 us
    gather x1, local copies, waits for them, and re-layouts, body(): gathered = rate_packed[:, jnp.where(react_flags == 1, slot_index, 0)]  29.2 us
    scatter x1, local copies, waits for them, and re-layouts, body(): jnp.zeros((COMPS, capacity), jnp.bfloat16).at[:, slot_index]  21.7 us
    scatter-add x1, other arithmetic, body(): jax.ops.segment_sum(push_values, panel_ids, num_segments=panels_all)  14 us
    div x3, other arithmetic, weno_face(): (weight_zero * cand_zero + weight_one * cand_one + weight_two * cand_two)...  9.43 us
    ppermute x3, starting transfers between devices, extended(): after = lax.ppermute(initial, axis, down)  8.07 us
    unnamed x38, local copies, waits for them, and re-layouts  7.94 us
  transfers between devices with their start and end apart: 6, of which 2 were waited for; matrix products, arithmetic and copies ran while one was open for 24% of the time, Pallas kernels for 0%

profile of v1, /device:TPU:1, one launch (start us, length us, event | category | flops | bytes accessed | tf_op | source)
XLA Modules:
  0.0 372.8 jit_solution(12230809834034627826)
XLA Ops:
  0.6 0.9 convert_bitcast_fusion.3
  1.6 0.9 convert_bitcast_fusion.1
  2.5 1.0 convert_bitcast_fusion
  3.5 0.8 convert_bitcast_fusion.2
  4.3 0.8 fusion.173
  5.1 5.0 %collective-permute-start = (f32[12,3,8,128]{3,2,1,0:T(8,128)}, f32[12,3,8,128]{3,2,1,0:T(8,128)}, u32[]{:S(2)}, u32[]{:S(2)}) collective-permute-start(f32[12,3,8,128]{3,2,1,0:T(8,128)} %get-tuple-element.138), channel_id=1, source_target_pairs={{0,16},{16,32},{32,48},{48,64},{64,80},{80,96},{96,112},{112,128},... | collective-permute-start | bytes 442376 | tf_op jit(solution)/shard_map/ppermute | solution.py:22
  10.2 1.3 collective-permute-start.1
  11.5 0.8 fusion.171
  12.3 0.5 iota_compare_fusion.1
  12.8 0.5 compare_select_fusion.7
  13.4 0.6 iota_compare_fusion.2
  13.9 0.9 fusion.172
  14.8 0.6 compare_select_fusion.5
  15.6 0.9 maximum_bitcast_fusion
  16.5 2.7 copy.63
  19.5 0.7 slice.440
  20.2 0.9 reduce-window.12
  21.3 0.3 compare_select_fusion
  21.6 21.7 %scatter_custom_fusion = bf16[12,256]{0,1:T(8,128)(2,1)} fusion(s32[8192]{0:T(1024)S(1)} %bitcast.214, bf16[8192,12]{1,0:T(8,128)(2,1)} %copy.63, bf16[]{:T(256)} %constant.78.clone.1), kind=kCustom, calls=%fused_computation.316 | custom fusion | bytes 6656 | tf_op jit(solution)/shard_map/scatter | solution.py:274
  43.3 3.2 fusion.16
  46.5 1.8 fusion.8
  48.3 0.5 iota_compare_fusion
  48.8 1.8 rev.23
  50.6 1.8 rev.24
  52.4 1.9 rev.25
  54.3 0.9 rev.26
  55.4 29.2 %gather_fusion = bf16[8192,12]{1,0:T(8,128)(2,1)} fusion(bf16[12,256]{0,1:T(8,128)(2,1)S(1)} %copy.64, s32[8192]{0:T(1024)S(1)} %broadcast_clamp_fusion), kind=kCustom, calls=%fused_computation | custom fusion | bytes 425984 | tf_op jit(solution)/shard_map/gather | solution.py:277
  84.6 3.8 %convert_element_type.31 = f32[8192,12]{1,0:T(8,128)} convert(bf16[8192,12]{1,0:T(8,128)(2,1)} %gather_fusion) | non-fusion elementwise | flops 98304 | bytes 589824 | tf_op jit(solution)/shard_map/convert_element_type | solution.py:278
  88.4 3.6 copy.66
  91.9 0.6 pad_add_fusion
  92.6 1.2 multiply_select_fusion.2
  93.8 1.9 add_divide_fusion.2
  95.8 1.0 pad_maximum_fusion.5
  97.0 3.1 collective-permute-start.2
  100.2 1.5 collective-permute-start.3
  102.0 0.4 copy-done.14
  102.8 1.9 collective-permute-done.2
  104.9 3.7 %collective-permute-done.3 = f32[12,14,3,128]{3,1,2,0:T(8,128)S(1)} collective-permute-done((f32[12,14,3,128]{3,1,2,0:T(8,128)S(1)}, f32[12,14,3,128]{3,1,2,0:T(8,128)S(1)}, u32[]{:S(2)}, u32[]{:S(2)}) %collective-permute-start.3) | collective-permute-done | bytes 258080 | tf_op jit(solution)/shard_map/ppermute | solution.py:23
  108.9 0.5 copy-done.4
  109.7 3.6 add_divide_fusion.1
  113.8 0.3 slice_multiply_fusion.6
  114.1 0.3 copy-done.13
  114.6 0.5 fusion.22
  115.2 0.9 copy-done.1
  116.0 14.0 %scatter_custom_fusion.1 = f32[4096]{0:T(1024)S(1)} fusion(s32[2048]{0:T(1024)} %pad_add_fusion, f32[2048]{0:T(1024)S(1)} %pad_maximum_fusion.9, f32[]{:T(128)} %constant.54.clone.1), kind=kCustom, calls=%fused_computation.342 | custom fusion | flops 2048 | bytes 16896 | tf_op jit(solution)/shard_map/scatter-add | solution.py:293
  130.1 51.3 %psum.14 = f32[4096]{0:T(1024)S(1)} all-reduce(f32[4096]{0:T(1024)S(1)} %scatter_custom_fusion.1), channel_id=1, replica_groups=mesh['gx'=32,'gy'=4,'gz'=4] {'gy','gz'}, use_global_device_ids=true, to_apply=%region_11.12 | all-reduce | flops 4096 | bytes 32768 | tf_op jit(solution)/shard_map/psum | solution.py:294
  181.4 127.0 %psum.15 = f32[4096]{0:T(1024)S(1)} all-reduce(f32[4096]{0:T(1024)S(1)} %psum.14), channel_id=1, replica_groups=mesh['gx'=32,'gy'=4,'gz'=4] {'gx'}, use_global_device_ids=true, to_apply=%region_12.13 | all-reduce | flops 4096 | bytes 32768 | tf_op jit(solution)/shard_map/psum | solution.py:294
  308.3 1.5 pad_maximum_fusion
  309.8 2.0 fusion.169
  311.8 3.4 copy.59
  315.2 30.9 %collective-permute-start.4 = (f32[12,14,14,3]{2,1,3,0:T(8,128)}, f32[12,14,14,3]{2,1,3,0:T(8,128)}, u32[]{:S(2)}, u32[]{:S(2)}) collective-permute-start(f32[12,14,14,3]{2,1,3,0:T(8,128)} %copy.59), channel_id=1, source_target_pairs={{0,1},{1,2},{2,3},{4,5},{5,6},{6,7},{8,9},{9,10},{10,11},{12,13},{... | collective-permute-start | bytes 84680 | tf_op jit(solution)/shard_map/ppermute | solution.py:22
  346.2 3.4 copy.61
  349.5 5.3 %collective-permute-start.5 = (f32[12,14,14,3]{2,1,3,0:T(8,128)}, f32[12,14,14,3]{2,1,3,0:T(8,128)}, u32[]{:S(2)}, u32[]{:S(2)}) collective-permute-start(f32[12,14,14,3]{2,1,3,0:T(8,128)} %copy.61), channel_id=1, source_target_pairs={{1,0},{2,1},{3,2},{5,4},{6,5},{7,6},{9,8},{10,9},{11,10},{13,12},{... | collective-permute-start | bytes 84680 | tf_op jit(solution)/shard_map/ppermute | solution.py:23
  354.9 0.6 dynamic-slice_multiply_fusion
  355.5 1.7 slice.418
  357.2 2.3 copy.67
  359.5 1.7 slice.424
  361.2 2.3 copy.68
  363.5 1.5 multiply_select_fusion
  365.3 3.9 %add_divide_fusion = (f32[12,8,8,129]{3,2,1,0:T(8,128)S(1)}, f32[12,8,8,129]{3,2,1,0:T(8,128)S(1)}) fusion(f32[12,8,8,131]{3,2,1,0:T(8,128)S(1)} %get-tuple-element.134, f32[12,8,8,131]{3,2,1,0:T(8,128)S(1)} %get-tuple-element.135), kind=kLoop, calls=%fused_computation.53 | loop fusion | flops 12284928 | bytes 3170304 | tf_op jit(solution)/shard_map/div | solution.py:52
  369.7 0.3 slice_multiply_fusion
  370.5 0.5 fusion.24
  371.0 0.6 copy-done.2
  371.8 1.0 fusion.113
  (88 shorter events, 4.6 us)
Async XLA Ops:
  0.6 42.7 %copy-start = (bf16[800,1600]{1,0:T(8,128)(2,1)S(1)}, bf16[800,1600]{1,0:T(8,128)(2,1)}, u32[]{:S(2)}) copy-start(bf16[800,1600]{1,0:T(8,128)(2,1)} %param.11) | copy-start | bytes 7680004
  4.3 11.0 %copy-start.10 = (s32[2,8,128]{2,1,0:T(8,128)S(1)}, s32[2,8,128]{2,1,0:T(8,128)}, u32[]{:S(2)}) copy-start(s32[2,8,128]{2,1,0:T(8,128)} %param.9) | copy-start | bytes 24580
  5.1 87.4 %collective-permute-start = (f32[12,3,8,128]{3,2,1,0:T(8,128)}, f32[12,3,8,128]{3,2,1,0:T(8,128)}, u32[]{:S(2)}, u32[]{:S(2)}) collective-permute-start(f32[12,3,8,128]{3,2,1,0:T(8,128)} %get-tuple-element.138), channel_id=1, source_target_pairs={{0,16},{16,32},{32,48},{48,64},{64,80},{80,96},{96,112},{112,128},... | collective-permute-start | bytes 442376 | tf_op jit(solution)/shard_map/ppermute | solution.py:22
  10.2 82.4 %collective-permute-start.1 = (f32[12,3,8,128]{3,2,1,0:T(8,128)}, f32[12,3,8,128]{3,2,1,0:T(8,128)}, u32[]{:S(2)}, u32[]{:S(2)}) collective-permute-start(f32[12,3,8,128]{3,2,1,0:T(8,128)} %get-tuple-element.139), channel_id=1, source_target_pairs={{16,0},{32,16},{48,32},{64,48},{80,64},{96,80},{112,96},{128,112},... | collective-permute-start | bytes 442376 | tf_op jit(solution)/shard_map/ppermute | solution.py:23
  15.4 3.8 %copy-start.9 = (s32[8,8,128]{2,1,0:T(8,128)S(1)}, s32[8,8,128]{2,1,0:T(8,128)}, u32[]{:S(2)}) copy-start(s32[8,8,128]{2,1,0:T(8,128)} %param.8) | copy-start | bytes 98308
  43.3 3.2 copy-start.16
  88.4 4.2 %copy-start.15 = (f32[12]{0:T(128)S(1)}, f32[12]{0:T(128)}, u32[]{:S(2)}) copy-start(f32[12]{0:T(128)} %compare_select_fusion.7) | copy-start | bytes 148
  97.0 7.7 %collective-permute-start.2 = (f32[12,14,3,128]{3,1,2,0:T(8,128)S(1)}, f32[12,14,3,128]{3,1,2,0:T(8,128)S(1)}, u32[]{:S(2)}, u32[]{:S(2)}) collective-permute-start(f32[12,14,3,128]{3,1,2,0:T(8,128)S(1)} %copy.53), channel_id=1, source_target_pairs={{0,4},{4,8},{8,12},{1,5},{5,9},{9,13},{2,6},{6,10},{10,14},{3,7},{... | collective-permute-start | bytes 774152 | tf_op jit(solution)/shard_map/ppermute | solution.py:22
  100.2 8.4 %collective-permute-start.3 = (f32[12,14,3,128]{3,1,2,0:T(8,128)S(1)}, f32[12,14,3,128]{3,1,2,0:T(8,128)S(1)}, u32[]{:S(2)}, u32[]{:S(2)}) collective-permute-start(f32[12,14,3,128]{3,1,2,0:T(8,128)S(1)} %copy.55), channel_id=1, source_target_pairs={{4,0},{8,4},{12,8},{5,1},{9,5},{13,9},{6,2},{10,6},{14,10},{7,3},{... | collective-permute-start | bytes 774152 | tf_op jit(solution)/shard_map/ppermute | solution.py:23
  101.8 0.7 copy-start.14
  102.5 6.2 %copy-start.7 = (f32[12,8,3,128]{3,2,1,0:T(4,128)S(1)}, f32[12,8,3,128]{3,2,1,0:T(4,128)}, u32[]{:S(2)}) copy-start(f32[12,8,3,128]{3,2,1,0:T(4,128)} %rev.23) | copy-start | bytes 442372
  102.5 6.2 %copy-start.8 = (f32[12,8,3,128]{3,2,1,0:T(4,128)S(1)}, f32[12,8,3,128]{3,2,1,0:T(4,128)}, u32[]{:S(2)}) copy-start(f32[12,8,3,128]{3,2,1,0:T(4,128)} %rev.24) | copy-start | bytes 442372
  104.8 4.1 %copy-start.3 = (f32[12,14,3,128]{3,2,1,0:T(4,128)}, f32[12,14,3,128]{3,2,1,0:T(4,128)S(1)}, u32[]{:S(2)}) copy-start(f32[12,14,3,128]{3,2,1,0:T(4,128)S(1)} %copy.54) | copy-start | bytes 774148
  108.8 0.7 copy-start.4
  113.8 0.7 copy-start.13
  115.1 0.9 copy-start.1
  315.2 40.3 %collective-permute-start.4 = (f32[12,14,14,3]{2,1,3,0:T(8,128)}, f32[12,14,14,3]{2,1,3,0:T(8,128)}, u32[]{:S(2)}, u32[]{:S(2)}) collective-permute-start(f32[12,14,14,3]{2,1,3,0:T(8,128)} %copy.59), channel_id=1, source_target_pairs={{0,1},{1,2},{2,3},{4,5},{5,6},{6,7},{8,9},{9,10},{10,11},{12,13},{... | collective-permute-start | bytes 84680 | tf_op jit(solution)/shard_map/ppermute | solution.py:22
  346.1 17.3 %copy-start.12 = (f32[12]{0:T(128)S(1)}, f32[12]{0:T(128)}, u32[]{:S(2)}) copy-start(f32[12]{0:T(128)} %compare_select_fusion.5) | copy-start | bytes 148
  349.5 9.9 %collective-permute-start.5 = (f32[12,14,14,3]{2,1,3,0:T(8,128)}, f32[12,14,14,3]{2,1,3,0:T(8,128)}, u32[]{:S(2)}, u32[]{:S(2)}) collective-permute-start(f32[12,14,14,3]{2,1,3,0:T(8,128)} %copy.61), channel_id=1, source_target_pairs={{1,0},{2,1},{3,2},{5,4},{6,5},{7,6},{9,8},{10,9},{11,10},{13,12},{... | collective-permute-start | bytes 84680 | tf_op jit(solution)/shard_map/ppermute | solution.py:23
  369.7 0.6 copy-start.11
  370.5 1.1 copy-start.2
  370.5 1.2 copy-start.5
  370.5 1.3 copy-start.6
